TPU v7x, 32 devices: a whole 2x2x4 slice. The times are simulated.
32 devices in a mesh: section: 8 (over y, x, core), tensor: 4 (over z).
Axes of the slice: x: 2, y: 2, z: 4, core: 2. Of those that a mesh axis runs over, the one named last changes fastest.
Arguments:
- state: bfloat16 [8, 256, 6144], P('section', None, 'tensor'), may hold values from -6 to 6
- ln_gain: float32 [8, 6144], P('section'), may hold values from 0.1 to 1.9
- w_qkv: bfloat16 [8, 6144, 3, 4096], P('section', None, None, 'tensor'), may hold values from -0.078125 to 0.078125
- qk_gain: float32 [8, 2, 128], P('section'), may hold values from 0.5 to 1.5
- w_out: bfloat16 [8, 4096, 6144], P('section', 'tensor'), may hold values from -1 to 1
Outputs:
- advanced: bfloat16 [8, 256, 6144], P('section', None, 'tensor')
All inputs are finite; a program needn't handle non-finite values.
Results may differ from a plain program's by a relative error of at most 0.03.
Values may be sent and summed in bfloat16 or wider, within the bound.
A program may use at most 192 MiB of HBM per device.

v0:
```python
import jax
import jax.numpy as jnp
from jax import lax
from jax.sharding import PartitionSpec as P

HD = 128
STEPS = 2


def passed_along(shard, axis, by):
    peers = lax.axis_size(axis)
    return lax.ppermute(shard, axis, [(i, (i + by) % peers) for i in range(peers)])


def layer_norm(values, gain):
    mean = jnp.mean(values, axis=-1, keepdims=True)
    squares = jnp.mean(values * values, axis=-1, keepdims=True)
    spread = squares - mean * mean
    return (values - mean) * lax.rsqrt(spread + 1e-06) * gain


def on_device(state, ln_gain, w_qkv, qk_gain, w_out):
    current = state[0]
    patches = current.shape[0]
    full_width = w_qkv.shape[1]
    head_cols = w_qkv.shape[3]
    local_heads = head_cols // HD
    qkv_flat = w_qkv[0].reshape(full_width, 3 * head_cols)
    out_local = w_out[0]
    gain_row = ln_gain[0]
    norm_gains = qk_gain[0]
    for step_index in range(STEPS):
        gathered = lax.all_gather(current, "tensor", axis=1, tiled=True)
        normed = layer_norm(gathered.astype(jnp.float32), gain_row).astype(jnp.bfloat16)
        projected = jnp.dot(normed, qkv_flat, preferred_element_type=jnp.float32)
        projected = projected.reshape(patches, 3, local_heads, HD)
        query = layer_norm(projected[:, 0], norm_gains[0]).astype(jnp.bfloat16)
        keys_all = layer_norm(projected[:, 1], norm_gains[1]).astype(jnp.bfloat16)
        value = projected[:, 2].astype(jnp.bfloat16)
        scores = jnp.einsum(
            "phe,qhe->hpq", query, keys_all, preferred_element_type=jnp.float32
        ) / jnp.sqrt(jnp.float32(HD))
        expo = jnp.exp(scores)
        attend = (expo / jnp.sum(expo, axis=-1, keepdims=True)).astype(jnp.bfloat16)
        mixed_rows = jnp.einsum("hpq,qhe->phe", attend, value, preferred_element_type=jnp.float32)
        mixed_rows = mixed_rows.astype(jnp.bfloat16).reshape(patches, head_cols)
        branch = lax.psum_scatter(
            lax.dot_general(
                out_local, mixed_rows, (((0,), (1,)), ((), ())), preferred_element_type=jnp.float32
            ).astype(jnp.bfloat16),
            "tensor",
            scatter_dimension=0,
            tiled=True,
        ).astype(jnp.float32)
        renewed = (current.astype(jnp.float32) + branch.T).astype(jnp.bfloat16)
        current = passed_along(renewed, "section", 1)
    return current[None]


def solution(mesh):
    placed = (
        P("section", None, "tensor"),
        P("section", None),
        P("section", None, None, "tensor"),
        P("section", None, None),
        P("section", "tensor", None),
    )
    return jax.shard_map(
        on_device,
        mesh=mesh,
        in_specs=placed,
        out_specs=P("section", None, "tensor"),
        check_vma=False,
    )
```

profile of v0, /device:TPU:0, one launch (start us, length us, event | category | flops | bytes accessed | tf_op | source)
XLA Modules:
  0.0 348.6 jit_solution(13225383114152515778)
XLA Ops:
  6.5 0.0 all-gather.6.cloned.1.call-start
  6.5 0.7 all-gather.6.cloned.1.call-update
  7.3 0.0 copy-start.4
  7.3 0.0 reduce-scatter.3.cloned.1.call-start
  7.3 48.9 %copy.12 = bf16[1,6144,3,1024]{1,3,2,0:T(8,128)(2,1)} copy(bf16[1,6144,3,1024]{3,1,2,0:T(8,128)(2,1)} %param.7) | data formatting | bytes 75497472 | tf_op args[2]
  56.2 0.0 copy-done.4
  56.2 18.9 %all-gather.6.cloned.1.call-done = bf16[1,256,6144]{2,1,0:T(8,128)(2,1)} async-done(((bf16[1,256,1536]{2,1,0:T(8,128)(2,1)}), bf16[1,256,6144]{2,1,0:T(8,128)(2,1)}) %all-gather.6.cloned.1.call-update) | async-done | bytes 3145744 | tf_op jit(solution)/shard_map/all_gather | solution.py:33
  75.1 2.5 convert_reduce_fusion.1
  77.7 0.3 copy-done
  78.0 0.7 fusion.18
  78.7 0.0 slice-start.1
  78.7 0.0 slice-start.2
  78.7 18.4 %fusion.30 = f32[256,3,8,128]{0,3,2,1:T(8,128)S(1)} fusion(bf16[3,8,128,6144]{3,2,1,0:T(8,128)(2,1)} %bitcast.140, bf16[1,256,6144]{2,1,0:T(8,128)(2,1)} %all-gather.6.cloned.1.call-done, f32[6144]{0:T(1024)S(1)} %bitcast.145, f32[256]{0:T(256)S(1)} %get-tuple-element.28, f32[256]{0:T(256)S(1)} %get-tuple-element.27), kind=kOutput, calls=%fused_computation.26 | convolution fusion | flops 9671540736 | bytes 44066816 | tf_op jit(solution)/shard_map/dot_general | solution.py:35
  97.1 0.2 fusion.57
  97.3 0.2 slice_reduce_fusion.3
  97.5 0.7 fusion.38
  98.2 0.5 convolution_convert_fusion.1
  98.7 0.0 slice-done
  98.7 0.0 slice-done.1
  98.7 0.0 slice-done.2
  98.7 5.0 %fusion.15 = bf16[6144,256]{0,1:T(8,128)(2,1)} fusion(bf16[256,1024]{0,1:T(8,128)(2,1)S(1)} %bitcast.143, bf16[1,1024,6144]{2,1,0:T(8,128)(2,1)S(1)} %bitcast.137), kind=kOutput, calls=%fused_computation.14 | convolution fusion | flops 3222798336 | bytes 16252928 | tf_op jit(solution)/shard_map/dot_general | solution.py:48
  103.7 0.0 reduce-scatter.3.cloned.1.call-update
  103.7 0.0 all-gather.4.cloned.1.call-start
  103.8 59.0 %reduce-scatter.3.cloned.1.call-done = bf16[1536,256]{0,1:T(8,128)(2,1)} async-done(((bf16[6144,256]{0,1:T(8,128)(2,1)}), bf16[1536,256]{0,1:T(8,128)(2,1)}) %reduce-scatter.3.cloned.1.call-update) | async-done | bytes 786448 | tf_op jit(solution)/shard_map/reduce_scatter | solution.py:47
  162.8 0.0 copy-done.1
  162.8 1.3 fusion.40
  164.1 0.1 collective-permute-start
  164.2 12.3 %collective-permute-done = bf16[256,1536]{1,0:T(8,128)(2,1)S(1)} collective-permute-done((bf16[256,1536]{1,0:T(8,128)(2,1)S(1)}, bf16[256,1536]{1,0:T(8,128)(2,1)S(1)}, u32[]{:S(2)}, u32[]{:S(2)}) %collective-permute-start) | collective-permute-done | bytes 786464 | tf_op jit(solution)/shard_map/ppermute | solution.py:12
  176.5 0.9 copy-done.2
  177.4 0.0 all-gather.4.cloned.1.call-update
  177.4 0.2 reduce-scatter.5.cloned.1.call-start
  177.6 62.5 %all-gather.4.cloned.1.call-done = bf16[256,6144]{1,0:T(8,128)(2,1)} async-done(((bf16[256,1536]{1,0:T(8,128)(2,1)}), bf16[256,6144]{1,0:T(8,128)(2,1)}) %all-gather.4.cloned.1.call-update) | async-done | bytes 3145744 | tf_op jit(solution)/shard_map/all_gather | solution.py:33
  240.2 3.4 convert_reduce_fusion
  243.5 0.0 slice-start.4
  243.6 0.0 slice-start.5
  243.6 18.2 %fusion.27 = f32[256,3,8,128]{0,3,2,1:T(8,128)S(1)} fusion(bf16[3,8,128,6144]{3,2,1,0:T(8,128)(2,1)} %bitcast.141, bf16[256,6144]{1,0:T(8,128)(2,1)} %all-gather.4.cloned.1.call-done, f32[256]{0:T(256)S(1)} %get-tuple-element.24, f32[256]{0:T(256)S(1)} %get-tuple-element.23, f32[6144]{0:T(1024)S(1)} %bitcast.146), kind=kOutput, calls=%fused_computation.24 | convolution fusion | flops 9671540736 | bytes 44066816 | tf_op jit(solution)/shard_map/dot_general | solution.py:35
  261.8 0.2 fusion.49
  262.0 0.2 slice_reduce_fusion.1
  262.2 0.7 fusion.39
  262.8 0.5 convolution_convert_fusion
  263.4 5.0 %fusion.12 = bf16[6144,256]{0,1:T(8,128)(2,1)} fusion(bf16[256,1024]{0,1:T(8,128)(2,1)S(1)} %bitcast.144, bf16[1,1024,6144]{2,1,0:T(8,128)(2,1)S(1)} %bitcast.139), kind=kOutput, calls=%fused_computation.13 | convolution fusion | flops 3222798336 | bytes 16252928 | tf_op jit(solution)/shard_map/dot_general | solution.py:48
  268.4 0.0 reduce-scatter.5.cloned.1.call-update
  268.4 59.1 %reduce-scatter.5.cloned.1.call-done = bf16[1536,256]{0,1:T(8,128)(2,1)} async-done(((bf16[6144,256]{0,1:T(8,128)(2,1)}), bf16[1536,256]{0,1:T(8,128)(2,1)}) %reduce-scatter.5.cloned.1.call-update) | async-done | bytes 786448 | tf_op jit(solution)/shard_map/reduce_scatter | solution.py:47
  327.5 0.0 copy-done.3
  327.5 1.3 fusion.41
  328.8 0.1 collective-permute-start.1
  328.9 12.3 %collective-permute-done.1 = bf16[256,1536]{1,0:T(8,128)(2,1)S(1)} collective-permute-done((bf16[256,1536]{1,0:T(8,128)(2,1)S(1)}, bf16[256,1536]{1,0:T(8,128)(2,1)S(1)}, u32[]{:S(2)}, u32[]{:S(2)}) %collective-permute-start.1) | collective-permute-done | bytes 786464 | tf_op jit(solution)/shard_map/ppermute | solution.py:12
  341.2 0.9 copy.28
  (19 shorter events, 0.1 us)
Async XLA Ops:
  6.5 68.6 %all-gather.6.cloned.1.call-start = ((), (), s32[]{:S(2)}) async-start(), calls=%async_computation.5 | async-start | bytes 3932160 | tf_op jit(solution)/shard_map/all_gather | solution.py:33
  7.3 48.9 %copy-start.4 = (f32[1,2,128]{2,1,0:T(2,128)S(1)}, f32[1,2,128]{2,1,0:T(2,128)}, u32[]{:S(2)}) copy-start(f32[1,2,128]{2,1,0:T(2,128)} %param.8) | copy-start | bytes 3076
  7.3 155.6 %reduce-scatter.3.cloned.1.call-start = ((), (), s32[]{:S(2)}) async-start(), calls=%async_computation.2 | async-start | bytes 3932160 | tf_op jit(solution)/shard_map/reduce_scatter | solution.py:47
  75.1 2.8 copy-start
  75.1 3.6 %copy-start.5 = (f32[1,6144]{1,0:T(1,128)S(1)}, f32[1,6144]{1,0:T(1,128)}, u32[]{:S(2)}) copy-start(f32[1,6144]{1,0:T(1,128)} %param.6) | copy-start | bytes 73732
  78.0 20.7 %slice-start = ((s8[12582912]{0:T(1024)(128)(4,1)}), s8[4194304]{0:T(1024)(128)(4,1)S(1)}, s32[]{:S(2)}) async-start(s8[12582912]{0:T(1024)(128)(4,1)} %bitcast.136), calls=%async_computation.6 | async-start | bytes 8388608
  78.7 20.0 %slice-start.1 = ((s8[12582912]{0:T(1024)(128)(4,1)}), s8[4194304]{0:T(1024)(128)(4,1)S(1)}, s32[]{:S(2)}) async-start(s8[12582912]{0:T(1024)(128)(4,1)} %bitcast.136), calls=%async_computation.7 | async-start | bytes 8388608
  78.7 20.0 %slice-start.2 = ((s8[12582912]{0:T(1024)(128)(4,1)}), s8[4194304]{0:T(1024)(128)(4,1)S(1)}, s32[]{:S(2)}) async-start(s8[12582912]{0:T(1024)(128)(4,1)} %bitcast.136), calls=%async_computation.8 | async-start | bytes 8388608
  103.7 59.1 %copy-start.1 = (bf16[1,256,1536]{2,1,0:T(8,128)(2,1)S(1)}, bf16[1,256,1536]{2,1,0:T(8,128)(2,1)}, u32[]{:S(2)}) copy-start(bf16[1,256,1536]{2,1,0:T(8,128)(2,1)} %param.5) | copy-start | bytes 2359300
  103.7 136.4 %all-gather.4.cloned.1.call-start = ((), (), s32[]{:S(2)}) async-start(), calls=%async_computation.3 | async-start | bytes 3932160 | tf_op jit(solution)/shard_map/all_gather | solution.py:33
  164.1 12.4 %collective-permute-start = (bf16[256,1536]{1,0:T(8,128)(2,1)S(1)}, bf16[256,1536]{1,0:T(8,128)(2,1)S(1)}, u32[]{:S(2)}, u32[]{:S(2)}) collective-permute-start(bf16[256,1536]{1,0:T(8,128)(2,1)S(1)} %fusion.40), channel_id=1, source_target_pairs={{0,4},{4,8},{8,12},{12,16},{16,20},{20,24},{24,28},{28,0},{1,5},{5... | collective-permute-start | bytes 2359304 | tf_op jit(solution)/shard_map/ppermute | solution.py:12
  176.5 0.9 copy-start.2
  177.4 150.1 %reduce-scatter.5.cloned.1.call-start = ((), (), s32[]{:S(2)}) async-start(), calls=%async_computation.4 | async-start | bytes 3932160 | tf_op jit(solution)/shard_map/reduce_scatter | solution.py:47
  240.2 23.2 %slice-start.3 = ((s8[12582912]{0:T(1024)(128)(4,1)}), s8[4194304]{0:T(1024)(128)(4,1)S(1)}, s32[]{:S(2)}) async-start(s8[12582912]{0:T(1024)(128)(4,1)} %bitcast.138), calls=%async_computation.9 | async-start | bytes 8388608
  243.5 19.8 %slice-start.4 = ((s8[12582912]{0:T(1024)(128)(4,1)}), s8[4194304]{0:T(1024)(128)(4,1)S(1)}, s32[]{:S(2)}) async-start(s8[12582912]{0:T(1024)(128)(4,1)} %bitcast.138), calls=%async_computation.10 | async-start | bytes 8388608
  243.6 19.8 %slice-start.5 = ((s8[12582912]{0:T(1024)(128)(4,1)}), s8[4194304]{0:T(1024)(128)(4,1)S(1)}, s32[]{:S(2)}) async-start(s8[12582912]{0:T(1024)(128)(4,1)} %bitcast.138), calls=%async_computation.11 | async-start | bytes 8388608
  268.4 59.1 %copy-start.3 = (bf16[256,1536]{1,0:T(8,128)(2,1)S(1)}, bf16[256,1536]{1,0:T(8,128)(2,1)}, u32[]{:S(2)}) copy-start(bf16[256,1536]{1,0:T(8,128)(2,1)} %copy-done.2) | copy-start | bytes 2359300
  328.8 12.4 %collective-permute-start.1 = (bf16[256,1536]{1,0:T(8,128)(2,1)S(1)}, bf16[256,1536]{1,0:T(8,128)(2,1)S(1)}, u32[]{:S(2)}, u32[]{:S(2)}) collective-permute-start(bf16[256,1536]{1,0:T(8,128)(2,1)S(1)} %fusion.41), channel_id=1, source_target_pairs={{0,4},{4,8},{8,12},{12,16},{16,20},{20,24},{24,28},{28,0},{1,5},{5... | collective-permute-start | bytes 2359304 | tf_op jit(solution)/shard_map/ppermute | solution.py:12
Sparse Core Ops, SparseCore 0:
  8.9 66.1 all-gather.5
  103.8 58.9 reduce-scatter.2
  177.5 62.5 all-gather.3
  268.5 58.9 reduce-scatter.4
where the time goes:
time: 350 us; the launch traced here: 349 us
  waiting for transfers between devices  225 us (64%)
  local copies, waits for them, and re-layouts  51 us (15%)
  matrix products  48.9 us (14%)
  between operations  13.4 us (4%)
  other arithmetic  9.95 us (3%)
    reduce_scatter x2, waiting for transfers between devices, on_device(): lax.psum_scatter(lax.dot_general(out_local, mixed_rows, (((0,), (1,)), ((...  118 us
    all_gather x2, waiting for transfers between devices, on_device(): gathered = lax.all_gather(current, 'tensor', axis=1, tiled=True)  81.5 us
    unnamed x26, local copies, waits for them, and re-layouts  51 us
    dot_general x2, matrix products, on_device(): projected = jnp.dot(normed, qkv_flat, preferred_element_type=jnp.float32)  36.6 us
    ppermute x2, waiting for transfers between devices, passed_along(): lax.ppermute(shard, axis, [(i, (i + by) % peers) for i in range(peers)])  24.6 us
    dot_general x2, matrix products, on_device(): lax.dot_general(out_local, mixed_rows, (((0,), (1,)), ((), ())), preferre...  9.93 us
  transfers between devices with their start and end apart: 6, of which 6 were waited for; matrix products, arithmetic and copies ran while one was open for 14% of the time, Pallas kernels for 0%

commit v1 on v0

v1 whole, which is shorter than its diff:
```python
import functools

import jax
import jax.numpy as jnp
from jax import lax
from jax.experimental import pallas as pl
from jax.experimental.pallas import tpu as pltpu
from jax.sharding import PartitionSpec as P

HD = 128
STEPS = 2
CHUNKS = 4
MESH = pl.DeviceIdType.MESH


def layer_norm(values, gain):
    mean = jnp.mean(values, axis=-1, keepdims=True)
    squares = jnp.mean(values * values, axis=-1, keepdims=True)
    spread = squares - mean * mean
    return (values - mean) * lax.rsqrt(spread + 1e-06) * gain


def relay_kernel(
    n, sections, chunks, gathers,
    mixed_ref, x_ref, w_ref, out_ref,
    slots, part, renewed,
    rs_send, rs_recv, ag_send, ag_recv, shift_send, shift_recv,
):
    t = lax.axis_index("tensor")
    s = lax.axis_index("section")
    patches, width = x_ref.shape
    rows = patches // chunks
    following, previous = lax.rem(s + 1, sections), lax.rem(s + sections - 1, sections)
    has_left, has_right = t > 0, t < n - 1

    def span(c):
        return pl.ds(c * rows, rows)

    def columns(f):
        return pl.ds(pl.multiple_of(f * width, 128), width)

    def rs_right(c, f):
        return pltpu.make_async_remote_copy(
            src_ref=slots.at[c, f + 1], dst_ref=slots.at[c, f + 1],
            send_sem=rs_send.at[c, f + 1], recv_sem=rs_recv.at[c, f + 1],
            device_id=(s, t + 1), device_id_type=MESH)

    def rs_left(c, f):
        return pltpu.make_async_remote_copy(
            src_ref=slots.at[c, f], dst_ref=slots.at[c, f],
            send_sem=rs_send.at[c, f], recv_sem=rs_recv.at[c, f],
            device_id=(s, t - 1), device_id_type=MESH)

    def ag_copy(c, f, step):
        block = out_ref.at[span(c), columns(f)]
        return pltpu.make_async_remote_copy(
            src_ref=block, dst_ref=block,
            send_sem=ag_send.at[c, f if step > 0 else f + 1], recv_sem=ag_recv.at[c, f],
            device_id=(s, t + step), device_id_type=MESH)

    def shift(c):
        target = out_ref.at[span(c), columns(t)] if gathers else out_ref.at[span(c), :]
        return pltpu.make_async_remote_copy(
            src_ref=renewed.at[span(c), :], dst_ref=target,
            send_sem=shift_send.at[c], recv_sem=shift_recv.at[c],
            device_id=(following, t), device_id_type=MESH)

    def products(c):
        def one(f, carry):
            part[c % 2, f] = jnp.dot(
                mixed_ref[span(c), :], w_ref[:, columns(f)], preferred_element_type=jnp.float32)
            return carry
        lax.fori_loop(0, n, one, 0)

    def end_sends(c):
        def one(i, carry):
            @pl.when(jnp.logical_not(has_left))
            def _():
                f = n - 1 - i
                slots[c, f + 1] = part[c % 2, f].astype(jnp.bfloat16)
                rs_right(c, f).start()

            @pl.when(jnp.logical_not(has_right))
            def _():
                slots[c, i] = part[c % 2, i].astype(jnp.bfloat16)
                rs_left(c, i).start()
            return carry
        lax.fori_loop(0, n - 1, one, 0)

    def forward_right(c, i):
        f = n - 1 - i

        @pl.when(jnp.logical_and(has_left, f > t))
        def _():
            rs_right(c, f).wait_recv()
            total = slots[c, f + 1].astype(jnp.float32) + part[c % 2, f]
            slots[c, f + 1] = total.astype(jnp.bfloat16)
            rs_right(c, f).start()

    def forward_left(c, i):
        @pl.when(jnp.logical_and(has_right, i < t))
        def _():
            rs_left(c, i).wait_recv()
            total = slots[c, i].astype(jnp.float32) + part[c % 2, i]
            slots[c, i] = total.astype(jnp.bfloat16)
            rs_left(c, i).start()

    def ag_start(c):
        shift(c).wait_recv()

        @pl.when(has_right)
        def _():
            ag_copy(c, t, 1).start()

        @pl.when(has_left)
        def _():
            ag_copy(c, t, -1).start()

    def ag_forward(c, d):
        @pl.when(t - d >= 0)
        def _():
            ag_copy(c, t - d, 1).wait_recv()

            @pl.when(has_right)
            def _():
                ag_copy(c, t - d, 1).start()

        @pl.when(t + d < n)
        def _():
            ag_copy(c, t + d, -1).wait_recv()

            @pl.when(has_left)
            def _():
                ag_copy(c, t + d, -1).start()

    def finish(c):
        total = x_ref[span(c), :].astype(jnp.float32) + part[c % 2, t]
        renewed[span(c), :] = total.astype(jnp.bfloat16)

        def take(slot):
            rs_left(c, slot).wait_recv()
            part[c % 2, t] = part[c % 2, t] + slots[c, slot].astype(jnp.float32)

        @pl.when(has_left)
        def _():
            take(t + 1)

        @pl.when(has_right)
        def _():
            take(t)
        total = x_ref[span(c), :].astype(jnp.float32) + part[c % 2, t]
        renewed[span(c), :] = total.astype(jnp.bfloat16)
        shift(c).start()

    barrier = pltpu.get_barrier_semaphore()
    for section in (following, previous):
        pl.semaphore_signal(barrier, inc=1, device_id=(section, t), device_id_type=MESH)

    @pl.when(has_left)
    def _():
        pl.semaphore_signal(barrier, inc=1, device_id=(s, t - 1), device_id_type=MESH)

    @pl.when(has_right)
    def _():
        pl.semaphore_signal(barrier, inc=1, device_id=(s, t + 1), device_id_type=MESH)
    products(0)
    pl.semaphore_wait(barrier, 2 + has_left.astype(jnp.int32) + has_right.astype(jnp.int32))

    for c in range(chunks + 1):
        if c < chunks:
            end_sends(c)
            if c + 1 < chunks:
                products(c + 1)
        if gathers and c > 0:
            ag_start(c - 1)

        def step(i, carry):
            if c < chunks:
                @pl.when(2 * t < n)
                def _():
                    forward_right(c, i)
                    forward_left(c, i)

                @pl.when(2 * t >= n)
                def _():
                    forward_left(c, i)
                    forward_right(c, i)
            if gathers and c > 0:
                ag_forward(c - 1, i + 1)
            return carry
        lax.fori_loop(0, n - 1, step, 0)
        if c < chunks:
            finish(c)

    def drain(c, carry):
        if not gathers:
            shift(c).wait_recv()
        shift(c).wait_send()

        def one(f, inner):
            @pl.when(f > t)
            def _():
                rs_right(c, f).wait_send()

            @pl.when(f < t)
            def _():
                rs_left(c, f).wait_send()
            if gathers:
                @pl.when(jnp.logical_and(has_right, f <= t))
                def _():
                    ag_copy(c, f, 1).wait_send()

                @pl.when(jnp.logical_and(has_left, f >= t))
                def _():
                    ag_copy(c, f, -1).wait_send()
            return inner
        return lax.fori_loop(0, n, one, carry)
    lax.fori_loop(0, chunks, drain, 0)


def relay(mixed, x, w_out, gathers):
    n, sections = lax.axis_size("tensor"), lax.axis_size("section")
    patches, width = x.shape
    rows = patches // CHUNKS
    dma = pltpu.SemaphoreType.DMA
    vmem = pl.BlockSpec(memory_space=pltpu.VMEM)
    return pl.pallas_call(
        functools.partial(relay_kernel, n, sections, CHUNKS, gathers),
        out_shape=jax.ShapeDtypeStruct((patches, n * width if gathers else width), jnp.bfloat16),
        in_specs=[vmem] * 3,
        out_specs=vmem,
        scratch_shapes=[
            pltpu.VMEM((CHUNKS, n + 1, rows, width), jnp.bfloat16),
            pltpu.VMEM((2, n, rows, width), jnp.float32),
            pltpu.VMEM((patches, width), jnp.bfloat16),
            dma((CHUNKS, n + 1)), dma((CHUNKS, n + 1)),
            dma((CHUNKS, n + 1)), dma((CHUNKS, n)),
            dma((CHUNKS,)), dma((CHUNKS,)),
        ],
        cost_estimate=pl.CostEstimate(
            flops=2 * patches * w_out.shape[0] * w_out.shape[1],
            bytes_accessed=2 * w_out.size, transcendentals=0),
        compiler_params=pltpu.CompilerParams(
            collective_id=1 if gathers else 0, has_side_effects=True,
            vmem_limit_bytes=48 * 1024 * 1024),
        name="relay_and_gather" if gathers else "relay",
    )(mixed, x, w_out)


def on_device(state, ln_gain, w_qkv, qk_gain, w_out):
    current = state[0]
    patches, width = current.shape
    full_width = w_qkv.shape[1]
    head_cols = w_qkv.shape[3]
    local_heads = head_cols // HD
    qkv_flat = w_qkv[0].reshape(full_width, 3 * head_cols)
    out_local = w_out[0]
    gain_row = ln_gain[0]
    norm_gains = qk_gain[0]
    gathered = lax.all_gather(current, "tensor", axis=1, tiled=True)
    for step_index in range(STEPS):
        normed = layer_norm(gathered.astype(jnp.float32), gain_row).astype(jnp.bfloat16)
        projected = jnp.dot(normed, qkv_flat, preferred_element_type=jnp.float32)
        projected = projected.reshape(patches, 3, local_heads, HD)
        query = layer_norm(projected[:, 0], norm_gains[0]).astype(jnp.bfloat16)
        keys_all = layer_norm(projected[:, 1], norm_gains[1]).astype(jnp.bfloat16)
        value = projected[:, 2].astype(jnp.bfloat16)
        scores = jnp.einsum(
            "phe,qhe->hpq", query, keys_all, preferred_element_type=jnp.float32
        ) / jnp.sqrt(jnp.float32(HD))
        expo = jnp.exp(scores)
        attend = (expo / jnp.sum(expo, axis=-1, keepdims=True)).astype(jnp.bfloat16)
        mixed_rows = jnp.einsum("hpq,qhe->phe", attend, value, preferred_element_type=jnp.float32)
        mixed_rows = mixed_rows.astype(jnp.bfloat16).reshape(patches, head_cols)
        last = step_index == STEPS - 1
        gathered = relay(mixed_rows, current, out_local, not last)
        if not last:
            start = lax.axis_index("tensor") * width
            current = lax.dynamic_slice_in_dim(gathered, start, width, axis=1)
    return gathered[None]


def solution(mesh):
    placed = (
        P("section", None, "tensor"),
        P("section", None),
        P("section", None, None, "tensor"),
        P("section", None, None),
        P("section", "tensor", None),
    )
    return jax.shard_map(
        on_device,
        mesh=mesh,
        in_specs=placed,
        out_specs=P("section", None, "tensor"),
        check_vma=False,
    )
```

time: 350 us -> 321 us (0.917)
  waiting for transfers between devices: 225 us -> 19.7 us
  Pallas kernels: 0 us -> 189 us
  matrix products: 48.9 us -> 35.8 us
  local copies, waits for them, and re-layouts: 51 us -> 56.3 us
  other arithmetic: 9.95 us -> 5.27 us
    pallas_call x0 -> x2, Pallas kernels: none -> 189 us  [relay(): pl.pallas_call(functools.partial(relay_kernel, n, sections, CHUNKS, gathe...]
    reduce_scatter x2 -> x0, waiting for transfers between devices: 118 us -> none  [on_device(): lax.psum_scatter(lax.dot_general(out_local, mixed_rows, (((0,), (1,)), ((...]
    all_gather x2 -> x1, waiting for transfers between devices: 81.5 us -> 19 us  [on_device(): gathered = lax.all_gather(current, 'tensor', axis=1, tiled=True)]
    ppermute x2 -> x0, waiting for transfers between devices: 24.6 us -> none  [passed_along(): lax.ppermute(shard, axis, [(i, (i + by) % peers) for i in range(peers)])]
    dot_general x2 -> x0, matrix products: 9.93 us -> none  [on_device(): lax.dot_general(out_local, mixed_rows, (((0,), (1,)), ((), ())), preferre...]
    dot_general x2, matrix products: 36.6 us -> 32.7 us  [on_device(): projected = jnp.dot(normed, qkv_flat, preferred_element_type=jnp.float32)]
    unnamed x26 -> x14, local copies, waits for them, and re-layouts: 51 us -> 53.3 us
  transfers between devices with their start and end apart: 6 -> 1, of which waited for: 6 -> 1; matrix products, arithmetic and copies ran while one was open for 14% -> 15% of each run, Pallas kernels for 0% -> 0%
where the time goes in v1:
time: 321 us; the launch traced here: 320 us
  Pallas kernels  189 us (59%)
  local copies, waits for them, and re-layouts  56.3 us (18%)
  matrix products  35.8 us (11%)
  waiting for transfers between devices  19.7 us (6%)
  between operations  13.5 us (4%)
  other arithmetic  5.27 us (2%)
    pallas_call x2, Pallas kernels, relay(): pl.pallas_call(functools.partial(relay_kernel, n, sections, CHUNKS, gathe...  189 us
    unnamed x14, local copies, waits for them, and re-layouts  53.3 us
    dot_general x2, matrix products, on_device(): projected = jnp.dot(normed, qkv_flat, preferred_element_type=jnp.float32)  32.7 us
    all_gather x1, waiting for transfers between devices, on_device(): gathered = lax.all_gather(current, 'tensor', axis=1, tiled=True)  19 us
  transfers between devices with their start and end apart: 1, of which 1 were waited for; matrix products, arithmetic and copies ran while one was open for 15% of the time, Pallas kernels for 0%

profile of v1, /device:TPU:0, one launch (start us, length us, event | category | flops | bytes accessed | tf_op | source)
XLA Modules:
  0.0 319.7 jit_solution(10606105443724814022)
XLA Ops:
  6.5 0.0 all-gather.3.cloned.1.call-start
  6.5 0.7 all-gather.3.cloned.1.call-update
  7.3 0.0 copy-start.4
  7.3 48.9 %copy.14 = bf16[1,6144,3,1024]{1,3,2,0:T(8,128)(2,1)} copy(bf16[1,6144,3,1024]{3,1,2,0:T(8,128)(2,1)} %param.7) | data formatting | bytes 75497472 | tf_op args[2]
  56.1 0.0 copy-done.4
  56.1 19.0 %all-gather.3.cloned.1.call-done = bf16[1,256,6144]{2,1,0:T(8,128)(2,1)} async-done(((bf16[1,256,1536]{2,1,0:T(8,128)(2,1)}), bf16[1,256,6144]{2,1,0:T(8,128)(2,1)}) %all-gather.3.cloned.1.call-update) | async-done | bytes 3145744 | tf_op jit(solution)/shard_map/all_gather | solution.py:260
  75.1 0.0 copy-start.3
  75.1 0.0 copy-start.5
  75.1 2.5 convert_reduce_fusion.1
  77.7 0.3 copy-done.3
  78.0 0.7 fusion.2
  78.7 0.0 copy-done.5
  78.7 16.3 %fusion.14 = f32[256,3,8,128]{0,3,2,1:T(8,128)S(1)} fusion(bf16[3,8,128,6144]{3,2,1,0:T(8,128)(2,1)} %bitcast.114, bf16[1,256,6144]{2,1,0:T(8,128)(2,1)S(1)} %copy-done.3, f32[6144]{0:T(1024)S(1)} %bitcast.118, f32[256]{0:T(256)S(1)} %get-tuple-element.28, f32[256]{0:T(256)S(1)} %get-tuple-element.27), kind=kOutput, calls=%fused_computation.18 | convolution fusion | flops 9671540736 | bytes 44066816 | tf_op jit(solution)/shard_map/dot_general | solution.py:263
  95.0 0.2 slice_reduce_fusion.3
  95.2 0.2 fusion.39
  95.4 0.7 fusion.22
  96.1 0.5 convolution_convert_fusion.1
  96.6 1.0 copy.31.mixed_ref
  97.6 0.0 copy-start
  97.6 1.1 copy-done
  98.7 0.0 copy-start.2
  98.7 1.0 copy-done.2
  99.8 119.2 %relay_and_gather.1 = bf16[256,6144]{1,0:T(8,128)(2,1)S(1)} custom-call(bf16[256,1024]{1,0:T(8,128)(2,1)S(1)} %copy-done.2, bf16[256,1536]{1,0:T(8,128)(2,1)S(1)} %bitcast.110, bf16[1024,6144]{1,0:T(8,128)(2,1)} %bitcast.112), custom_call_target="tpu_custom_call" | custom-call | flops 3221225472 | bytes 12582912 | tf_op jit(solution)/shard_map/relay_and_gather/pallas_call | solution.py:227
  219.0 1.3 convert_reduce_fusion
  220.3 16.3 %fusion.11 = f32[256,3,8,128]{0,3,2,1:T(8,128)S(1)} fusion(bf16[3,8,128,6144]{3,2,1,0:T(8,128)(2,1)} %bitcast.115, bf16[256,6144]{1,0:T(8,128)(2,1)S(1)} %relay_and_gather.1, f32[256]{0:T(256)S(1)} %get-tuple-element.24, f32[256]{0:T(256)S(1)} %get-tuple-element.23, f32[6144]{0:T(1024)S(1)} %bitcast.119), kind=kOutput, calls=%fused_computation.16 | convolution fusion | flops 9671540736 | bytes 44066816 | tf_op jit(solution)/shard_map/dot_general | solution.py:263
  236.7 0.2 slice_reduce_fusion.1
  236.8 0.2 fusion.31
  237.0 0.7 fusion.23
  237.7 1.3 convolution_convert_fusion
  239.0 2.0 copy.32.mixed_ref
  241.1 0.1 constant_dynamic-slice_fusion.x_ref
  241.1 0.0 copy-start.1
  241.1 1.0 copy-done.1
  242.2 69.8 %relay.1 = bf16[256,1536]{1,0:T(8,128)(2,1)S(1)} custom-call(bf16[256,1024]{1,0:T(8,128)(2,1)S(1)} %copy-done.1, bf16[256,1536]{1,0:T(8,128)(2,1)S(1)} %constant_dynamic-slice_fusion.x_ref, bf16[1024,6144]{1,0:T(8,128)(2,1)} %bitcast.113), custom_call_target="tpu_custom_call" | custom-call | flops 3221225472 | bytes 12582912 | tf_op jit(solution)/shard_map/relay/pallas_call | solution.py:227
  312.0 0.9 copy.34
  (6 shorter events, 0.1 us)
Async XLA Ops:
  6.5 68.6 %all-gather.3.cloned.1.call-start = ((), (), s32[]{:S(2)}) async-start(), calls=%async_computation | async-start | bytes 3932160 | tf_op jit(solution)/shard_map/all_gather | solution.py:260
  7.3 48.9 %copy-start.4 = (f32[1,2,128]{2,1,0:T(2,128)S(1)}, f32[1,2,128]{2,1,0:T(2,128)}, u32[]{:S(2)}) copy-start(f32[1,2,128]{2,1,0:T(2,128)} %param.8) | copy-start | bytes 3076
  75.1 2.8 copy-start.3
  75.1 3.5 %copy-start.5 = (f32[1,6144]{1,0:T(1,128)S(1)}, f32[1,6144]{1,0:T(1,128)}, u32[]{:S(2)}) copy-start(f32[1,6144]{1,0:T(1,128)} %param.6) | copy-start | bytes 73732
  97.6 1.1 copy-start
  98.7 1.0 copy-start.2
  241.1 1.0 copy-start.1
Sparse Core Ops, SparseCore 0:
  8.9 66.1 all-gather.2

commit v2 on v1

--- a/solution.py
+++ b/solution.py
@@ -34,7 +34,7 @@
     has_left, has_right = t > 0, t < n - 1
 
     def span(c):
-        return pl.ds(c * rows, rows)
+        return pl.ds(pl.multiple_of(c * rows, rows), rows)
 
     def columns(f):
         return pl.ds(pl.multiple_of(f * width, 128), width)
@@ -67,7 +67,7 @@
 
     def products(c):
         def one(f, carry):
-            part[c % 2, f] = jnp.dot(
+            part[c % 3, f] = jnp.dot(
                 mixed_ref[span(c), :], w_ref[:, columns(f)], preferred_element_type=jnp.float32)
             return carry
         lax.fori_loop(0, n, one, 0)
@@ -77,12 +77,12 @@
             @pl.when(jnp.logical_not(has_left))
             def _():
                 f = n - 1 - i
-                slots[c, f + 1] = part[c % 2, f].astype(jnp.bfloat16)
+                slots[c, f + 1] = part[c % 3, f].astype(jnp.bfloat16)
                 rs_right(c, f).start()
 
             @pl.when(jnp.logical_not(has_right))
             def _():
-                slots[c, i] = part[c % 2, i].astype(jnp.bfloat16)
+                slots[c, i] = part[c % 3, i].astype(jnp.bfloat16)
                 rs_left(c, i).start()
             return carry
         lax.fori_loop(0, n - 1, one, 0)
@@ -93,7 +93,7 @@
         @pl.when(jnp.logical_and(has_left, f > t))
         def _():
             rs_right(c, f).wait_recv()
-            total = slots[c, f + 1].astype(jnp.float32) + part[c % 2, f]
+            total = slots[c, f + 1].astype(jnp.float32) + part[c % 3, f]
             slots[c, f + 1] = total.astype(jnp.bfloat16)
             rs_right(c, f).start()
 
@@ -101,7 +101,7 @@
         @pl.when(jnp.logical_and(has_right, i < t))
         def _():
             rs_left(c, i).wait_recv()
-            total = slots[c, i].astype(jnp.float32) + part[c % 2, i]
+            total = slots[c, i].astype(jnp.float32) + part[c % 3, i]
             slots[c, i] = total.astype(jnp.bfloat16)
             rs_left(c, i).start()
 
@@ -134,12 +134,9 @@
                 ag_copy(c, t + d, -1).start()
 
     def finish(c):
-        total = x_ref[span(c), :].astype(jnp.float32) + part[c % 2, t]
-        renewed[span(c), :] = total.astype(jnp.bfloat16)
-
         def take(slot):
             rs_left(c, slot).wait_recv()
-            part[c % 2, t] = part[c % 2, t] + slots[c, slot].astype(jnp.float32)
+            part[c % 3, t] = part[c % 3, t] + slots[c, slot].astype(jnp.float32)
 
         @pl.when(has_left)
         def _():
@@ -148,7 +145,7 @@
         @pl.when(has_right)
         def _():
             take(t)
-        total = x_ref[span(c), :].astype(jnp.float32) + part[c % 2, t]
+        total = x_ref[span(c), :].astype(jnp.float32) + part[c % 3, t]
         renewed[span(c), :] = total.astype(jnp.bfloat16)
         shift(c).start()
 
@@ -166,15 +163,19 @@
     products(0)
     pl.semaphore_wait(barrier, 2 + has_left.astype(jnp.int32) + has_right.astype(jnp.int32))
 
-    for c in range(chunks + 1):
-        if c < chunks:
-            end_sends(c)
-            if c + 1 < chunks:
-                products(c + 1)
-        if gathers and c > 0:
-            ag_start(c - 1)
+    end_sends(0)
+    products(1)
+    for c in range(chunks + n if gathers else chunks):
+        if c + 1 < chunks:
+            end_sends(c + 1)
 
         def step(i, carry):
+            if gathers:
+                older = c - 2 - i
+
+                @pl.when(jnp.logical_and(older >= 0, older < chunks))
+                def _():
+                    ag_forward(older, i + 1)
             if c < chunks:
                 @pl.when(2 * t < n)
                 def _():
@@ -185,10 +186,14 @@
                 def _():
                     forward_left(c, i)
                     forward_right(c, i)
-            if gathers and c > 0:
-                ag_forward(c - 1, i + 1)
+            if gathers and 0 < c <= chunks:
+                @pl.when(i == 0)
+                def _():
+                    ag_start(c - 1)
             return carry
         lax.fori_loop(0, n - 1, step, 0)
+        if c + 2 < chunks:
+            products(c + 2)
         if c < chunks:
             finish(c)
 
@@ -231,7 +236,7 @@
         out_specs=vmem,
         scratch_shapes=[
             pltpu.VMEM((CHUNKS, n + 1, rows, width), jnp.bfloat16),
-            pltpu.VMEM((2, n, rows, width), jnp.float32),
+            pltpu.VMEM((3, n, rows, width), jnp.float32),
             pltpu.VMEM((patches, width), jnp.bfloat16),
             dma((CHUNKS, n + 1)), dma((CHUNKS, n + 1)),
             dma((CHUNKS, n + 1)), dma((CHUNKS, n)),

time: 321 us -> 314 us (0.978)
  Pallas kernels: 189 us -> 182 us
    pallas_call x2, Pallas kernels: 189 us -> 182 us  [relay(): pl.pallas_call(functools.partial(relay_kernel, n, sections, CHUNKS, gathe...]
  transfers between devices with their start and end apart: 1 -> 1, of which waited for: 1 -> 1; matrix products, arithmetic and copies ran while one was open for 15% -> 16% of each run, Pallas kernels for 0% -> 0%
where the time goes in v2:
time: 314 us; the launch traced here: 313 us
  Pallas kernels  182 us (58%)
  local copies, waits for them, and re-layouts  56.3 us (18%)
  matrix products  35.8 us (11%)
  waiting for transfers between devices  19.7 us (6%)
  between operations  13.5 us (4%)
  other arithmetic  5.27 us (2%)
    pallas_call x2, Pallas kernels, relay(): pl.pallas_call(functools.partial(relay_kernel, n, sections, CHUNKS, gathe...  182 us
    unnamed x14, local copies, waits for them, and re-layouts  53.3 us
    dot_general x2, matrix products, on_device(): projected = jnp.dot(normed, qkv_flat, preferred_element_type=jnp.float32)  32.7 us
    all_gather x1, waiting for transfers between devices, on_device(): gathered = lax.all_gather(current, 'tensor', axis=1, tiled=True)  19 us
  transfers between devices with their start and end apart: 1, of which 1 were waited for; matrix products, arithmetic and copies ran while one was open for 16% of the time, Pallas kernels for 0%

profile of v2, /device:TPU:0, one launch (start us, length us, event | category | flops | bytes accessed | tf_op | source)
XLA Modules:
  0.0 312.7 jit_solution(4639605961736978629)
XLA Ops:
  6.5 0.0 all-gather.3.cloned.1.call-start
  6.5 0.7 all-gather.3.cloned.1.call-update
  7.3 0.0 copy-start.4
  7.3 48.9 %copy.14 = bf16[1,6144,3,1024]{1,3,2,0:T(8,128)(2,1)} copy(bf16[1,6144,3,1024]{3,1,2,0:T(8,128)(2,1)} %param.7) | data formatting | bytes 75497472 | tf_op args[2]
  56.1 0.0 copy-done.4
  56.1 19.0 %all-gather.3.cloned.1.call-done = bf16[1,256,6144]{2,1,0:T(8,128)(2,1)} async-done(((bf16[1,256,1536]{2,1,0:T(8,128)(2,1)}), bf16[1,256,6144]{2,1,0:T(8,128)(2,1)}) %all-gather.3.cloned.1.call-update) | async-done | bytes 3145744 | tf_op jit(solution)/shard_map/all_gather | solution.py:265
  75.1 0.0 copy-start.3
  75.1 0.0 copy-start.5
  75.1 2.5 convert_reduce_fusion.1
  77.7 0.3 copy-done.3
  78.0 0.7 fusion.2
  78.7 0.0 copy-done.5
  78.7 16.3 %fusion.14 = f32[256,3,8,128]{0,3,2,1:T(8,128)S(1)} fusion(bf16[3,8,128,6144]{3,2,1,0:T(8,128)(2,1)} %bitcast.114, bf16[1,256,6144]{2,1,0:T(8,128)(2,1)S(1)} %copy-done.3, f32[6144]{0:T(1024)S(1)} %bitcast.118, f32[256]{0:T(256)S(1)} %get-tuple-element.28, f32[256]{0:T(256)S(1)} %get-tuple-element.27), kind=kOutput, calls=%fused_computation.18 | convolution fusion | flops 9671540736 | bytes 44066816 | tf_op jit(solution)/shard_map/dot_general | solution.py:268
  95.0 0.2 slice_reduce_fusion.3
  95.2 0.2 fusion.39
  95.4 0.7 fusion.22
  96.1 0.5 convolution_convert_fusion.1
  96.6 1.0 copy.31.mixed_ref
  97.6 0.0 copy-start
  97.6 1.1 copy-done
  98.7 0.0 copy-start.2
  98.7 1.0 copy-done.2
  99.8 115.8 %relay_and_gather.1 = bf16[256,6144]{1,0:T(8,128)(2,1)S(1)} custom-call(bf16[256,1024]{1,0:T(8,128)(2,1)S(1)} %copy-done.2, bf16[256,1536]{1,0:T(8,128)(2,1)S(1)} %bitcast.110, bf16[1024,6144]{1,0:T(8,128)(2,1)} %bitcast.112), custom_call_target="tpu_custom_call" | custom-call | flops 3221225472 | bytes 12582912 | tf_op jit(solution)/shard_map/relay_and_gather/pallas_call | solution.py:232
  215.6 1.3 convert_reduce_fusion
  216.9 16.3 %fusion.11 = f32[256,3,8,128]{0,3,2,1:T(8,128)S(1)} fusion(bf16[3,8,128,6144]{3,2,1,0:T(8,128)(2,1)} %bitcast.115, bf16[256,6144]{1,0:T(8,128)(2,1)S(1)} %relay_and_gather.1, f32[256]{0:T(256)S(1)} %get-tuple-element.24, f32[256]{0:T(256)S(1)} %get-tuple-element.23, f32[6144]{0:T(1024)S(1)} %bitcast.119), kind=kOutput, calls=%fused_computation.16 | convolution fusion | flops 9671540736 | bytes 44066816 | tf_op jit(solution)/shard_map/dot_general | solution.py:268
  233.2 0.2 slice_reduce_fusion.1
  233.4 0.2 fusion.31
  233.6 0.7 fusion.23
  234.3 1.3 convolution_convert_fusion
  235.6 2.0 copy.32.mixed_ref
  237.6 0.1 constant_dynamic-slice_fusion.x_ref
  237.7 0.0 copy-start.1
  237.7 1.0 copy-done.1
  238.7 66.2 %relay.1 = bf16[256,1536]{1,0:T(8,128)(2,1)S(1)} custom-call(bf16[256,1024]{1,0:T(8,128)(2,1)S(1)} %copy-done.1, bf16[256,1536]{1,0:T(8,128)(2,1)S(1)} %constant_dynamic-slice_fusion.x_ref, bf16[1024,6144]{1,0:T(8,128)(2,1)} %bitcast.113), custom_call_target="tpu_custom_call" | custom-call | flops 3221225472 | bytes 12582912 | tf_op jit(solution)/shard_map/relay/pallas_call | solution.py:232
  304.9 0.9 copy.34
  (6 shorter events, 0.1 us)
Async XLA Ops:
  6.5 68.6 %all-gather.3.cloned.1.call-start = ((), (), s32[]{:S(2)}) async-start(), calls=%async_computation | async-start | bytes 3932160 | tf_op jit(solution)/shard_map/all_gather | solution.py:265
  7.3 48.9 %copy-start.4 = (f32[1,2,128]{2,1,0:T(2,128)S(1)}, f32[1,2,128]{2,1,0:T(2,128)}, u32[]{:S(2)}) copy-start(f32[1,2,128]{2,1,0:T(2,128)} %param.8) | copy-start | bytes 3076
  75.1 2.8 copy-start.3
  75.1 3.5 %copy-start.5 = (f32[1,6144]{1,0:T(1,128)S(1)}, f32[1,6144]{1,0:T(1,128)}, u32[]{:S(2)}) copy-start(f32[1,6144]{1,0:T(1,128)} %param.6) | copy-start | bytes 73732
  97.6 1.1 copy-start
  98.7 1.0 copy-start.2
  237.7 1.0 copy-start.1
Sparse Core Ops, SparseCore 0:
  8.9 66.1 all-gather.2

commit v3 on v2

--- a/solution.py
+++ b/solution.py
@@ -9,7 +9,7 @@
 
 HD = 128
 STEPS = 2
-CHUNKS = 4
+CHUNKS = 8
 MESH = pl.DeviceIdType.MESH
 
 

time: 314 us -> 334 us (1.064)
  Pallas kernels: 182 us -> 202 us
    pallas_call x2, Pallas kernels: 182 us -> 202 us  [relay(): pl.pallas_call(functools.partial(relay_kernel, n, sections, CHUNKS, gathe...]
  transfers between devices with their start and end apart: 1 -> 1, of which waited for: 1 -> 1; matrix products, arithmetic and copies ran while one was open for 16% -> 15% of each run, Pallas kernels for 0% -> 0%
where the time goes in v3:
time: 334 us; the launch traced here: 332 us
  Pallas kernels  202 us (60%)
  local copies, waits for them, and re-layouts  56.3 us (17%)
  matrix products  35.8 us (11%)
  waiting for transfers between devices  19.7 us (6%)
  between operations  13.5 us (4%)
  other arithmetic  5.27 us (2%)
    pallas_call x2, Pallas kernels, relay(): pl.pallas_call(functools.partial(relay_kernel, n, sections, CHUNKS, gathe...  202 us
    unnamed x14, local copies, waits for them, and re-layouts  53.3 us
    dot_general x2, matrix products, on_device(): projected = jnp.dot(normed, qkv_flat, preferred_element_type=jnp.float32)  32.7 us
    all_gather x1, waiting for transfers between devices, on_device(): gathered = lax.all_gather(current, 'tensor', axis=1, tiled=True)  19 us
  transfers between devices with their start and end apart: 1, of which 1 were waited for; matrix products, arithmetic and copies ran while one was open for 15% of the time, Pallas kernels for 0%

profile of v3, /device:TPU:0, one launch (start us, length us, event | category | flops | bytes accessed | tf_op | source)
XLA Modules:
  0.0 332.3 jit_solution(5496748181826332422)
XLA Ops:
  6.5 0.0 all-gather.3.cloned.1.call-start
  6.5 0.7 all-gather.3.cloned.1.call-update
  7.3 0.0 copy-start.4
  7.3 48.9 %copy.14 = bf16[1,6144,3,1024]{1,3,2,0:T(8,128)(2,1)} copy(bf16[1,6144,3,1024]{3,1,2,0:T(8,128)(2,1)} %param.7) | data formatting | bytes 75497472 | tf_op args[2]
  56.1 0.0 copy-done.4
  56.1 19.0 %all-gather.3.cloned.1.call-done = bf16[1,256,6144]{2,1,0:T(8,128)(2,1)} async-done(((bf16[1,256,1536]{2,1,0:T(8,128)(2,1)}), bf16[1,256,6144]{2,1,0:T(8,128)(2,1)}) %all-gather.3.cloned.1.call-update) | async-done | bytes 3145744 | tf_op jit(solution)/shard_map/all_gather | solution.py:265
  75.1 0.0 copy-start.3
  75.1 0.0 copy-start.5
  75.1 2.5 convert_reduce_fusion.1
  77.7 0.3 copy-done.3
  78.0 0.7 fusion.2
  78.7 0.0 copy-done.5
  78.7 16.3 %fusion.14 = f32[256,3,8,128]{0,3,2,1:T(8,128)S(1)} fusion(bf16[3,8,128,6144]{3,2,1,0:T(8,128)(2,1)} %bitcast.114, bf16[1,256,6144]{2,1,0:T(8,128)(2,1)S(1)} %copy-done.3, f32[6144]{0:T(1024)S(1)} %bitcast.118, f32[256]{0:T(256)S(1)} %get-tuple-element.28, f32[256]{0:T(256)S(1)} %get-tuple-element.27), kind=kOutput, calls=%fused_computation.18 | convolution fusion | flops 9671540736 | bytes 44066816 | tf_op jit(solution)/shard_map/dot_general | solution.py:268
  95.0 0.2 slice_reduce_fusion.3
  95.2 0.2 fusion.39
  95.4 0.7 fusion.22
  96.1 0.5 convolution_convert_fusion.1
  96.6 1.0 copy.31.mixed_ref
  97.6 0.0 copy-start
  97.6 1.1 copy-done
  98.7 0.0 copy-start.2
  98.7 1.0 copy-done.2
  99.8 124.1 %relay_and_gather.1 = bf16[256,6144]{1,0:T(8,128)(2,1)S(1)} custom-call(bf16[256,1024]{1,0:T(8,128)(2,1)S(1)} %copy-done.2, bf16[256,1536]{1,0:T(8,128)(2,1)S(1)} %bitcast.110, bf16[1024,6144]{1,0:T(8,128)(2,1)} %bitcast.112), custom_call_target="tpu_custom_call" | custom-call | flops 3221225472 | bytes 12582912 | tf_op jit(solution)/shard_map/relay_and_gather/pallas_call | solution.py:232
  223.9 1.3 convert_reduce_fusion
  225.3 16.3 %fusion.11 = f32[256,3,8,128]{0,3,2,1:T(8,128)S(1)} fusion(bf16[3,8,128,6144]{3,2,1,0:T(8,128)(2,1)} %bitcast.115, bf16[256,6144]{1,0:T(8,128)(2,1)S(1)} %relay_and_gather.1, f32[256]{0:T(256)S(1)} %get-tuple-element.24, f32[256]{0:T(256)S(1)} %get-tuple-element.23, f32[6144]{0:T(1024)S(1)} %bitcast.119), kind=kOutput, calls=%fused_computation.16 | convolution fusion | flops 9671540736 | bytes 44066816 | tf_op jit(solution)/shard_map/dot_general | solution.py:268
  241.6 0.2 slice_reduce_fusion.1
  241.7 0.2 fusion.31
  241.9 0.7 fusion.23
  242.6 1.3 convolution_convert_fusion
  243.9 2.0 copy.32.mixed_ref
  246.0 0.1 constant_dynamic-slice_fusion.x_ref
  246.0 0.0 copy-start.1
  246.0 1.0 copy-done.1
  247.1 77.5 %relay.1 = bf16[256,1536]{1,0:T(8,128)(2,1)S(1)} custom-call(bf16[256,1024]{1,0:T(8,128)(2,1)S(1)} %copy-done.1, bf16[256,1536]{1,0:T(8,128)(2,1)S(1)} %constant_dynamic-slice_fusion.x_ref, bf16[1024,6144]{1,0:T(8,128)(2,1)} %bitcast.113), custom_call_target="tpu_custom_call" | custom-call | flops 3221225472 | bytes 12582912 | tf_op jit(solution)/shard_map/relay/pallas_call | solution.py:232
  324.6 0.9 copy.34
  (6 shorter events, 0.1 us)
Async XLA Ops:
  6.5 68.6 %all-gather.3.cloned.1.call-start = ((), (), s32[]{:S(2)}) async-start(), calls=%async_computation | async-start | bytes 3932160 | tf_op jit(solution)/shard_map/all_gather | solution.py:265
  7.3 48.9 %copy-start.4 = (f32[1,2,128]{2,1,0:T(2,128)S(1)}, f32[1,2,128]{2,1,0:T(2,128)}, u32[]{:S(2)}) copy-start(f32[1,2,128]{2,1,0:T(2,128)} %param.8) | copy-start | bytes 3076
  75.1 2.8 copy-start.3
  75.1 3.5 %copy-start.5 = (f32[1,6144]{1,0:T(1,128)S(1)}, f32[1,6144]{1,0:T(1,128)}, u32[]{:S(2)}) copy-start(f32[1,6144]{1,0:T(1,128)} %param.6) | copy-start | bytes 73732
  97.6 1.1 copy-start
  98.7 1.0 copy-start.2
  246.0 1.0 copy-start.1
Sparse Core Ops, SparseCore 0:
  8.9 66.1 all-gather.2
